TPU v7x, 32 devices: a whole 2x2x4 slice. The times are simulated.
32 devices in a mesh: groups: 2 (over y), map: 16 (over z, x, core).
Axes of the slice: x: 2, y: 2, z: 4, core: 2. Of those that a mesh axis runs over, the one named last changes fastest.
Arguments:
- amplitude_maps: bfloat16 [400, 512, 512], P('groups', 'map'), parts along dimension 0, may hold values from -6 to 6
- kept_blocks: int32 [512], P(('groups', 'map')), parts along dimension 0, may hold values from 0 to 2047, as said below
- block_owner: int32 [512, 1], P(('groups', 'map')), parts along dimension 0, may hold values from 0 to 15; in each aligned block of 16 rows (0 to 15, 16 to 31, ...) at most 2 rows name the same one
- observed: bfloat16 [8192], P(('groups', 'map')), parts along dimension 0, may hold values from -8 to 8
- error_scale: bfloat16 [8192], P(('groups', 'map')), parts along dimension 0, may hold values from 0.5 to 1.59375
- perturbation: bfloat16 [8192, 200], P(('groups', 'map')), parts along dimension 0, may hold values from -6 to 6
- model_slab: bfloat16 [200, 393216], P(None, ('groups', 'map')), parts along dimension 1, may hold values from -6 to 6
Outputs:
- updated_slab: bfloat16 [200, 393216], P(None, ('groups', 'map')), parts along dimension 1
- update_weights: float32 [400, 200], P('groups'), parts along dimension 0
- data_misfit: float32 [8192], P(('groups', 'map')), parts along dimension 0
There are 2 independent parts, one for each index of `groups`. A program takes and returns all parts, laid end to end along the dimension named above; each array names one. Nothing has to cross between parts.
Inputs may be any that keep to these rules, and one draw needn't show every extreme that they name: `kept_blocks`: the 16 entries of one device are distinct numbers of that device's own 2048 blocks. `block_owner`: at most 2 of the 16 kept blocks of one device share an owner.
All inputs are finite; a program needn't handle non-finite values.
Results may differ from a plain program's by a relative error of at most 0.0018.
The roundings to bfloat16 on the way count: a program that leaves them out, or rounds other values in their place, can miss the bound.
Values may be sent and summed in bfloat16 or wider, within the bound.
A program may use at most 128 MiB of HBM per device.

v0:
```python
import math

import jax
import jax.numpy as jnp
from jax import lax
from jax.sharding import PartitionSpec as P

BLK = 8
CAP = 2


inflation = 4.0
epsilon = 1e-06


def dct_table(length):
    frequency = jnp.arange(length, dtype=jnp.float32)[:, None]
    sample = jnp.arange(length, dtype=jnp.float32)[None, :]
    cosine_table = jnp.cos(math.pi * (2.0 * sample + 1.0) * frequency / (2.0 * length))
    factor = jnp.where(frequency == 0, math.sqrt(1.0 / length), math.sqrt(2.0 / length))
    return (cosine_table * factor).astype(jnp.bfloat16)


def gram_terms(predicted, observed_rows, scale_rows, noise_rows, live_mask, weight_scale):
    members = predicted.shape[1]
    center = jnp.mean(predicted, axis=1, keepdims=True)
    anomaly = (predicted - center) / math.sqrt(members - 1)
    weight = live_mask * weight_scale / (scale_rows * scale_rows)
    mismatch = (
        observed_rows[:, None] + math.sqrt(inflation) * scale_rows[:, None] * noise_rows - predicted
    )
    weighted = anomaly * weight[:, None]
    contract = (((0,), (0,)), ((), ()))
    gram_matrix = lax.dot_general(anomaly, weighted, contract, precision=lax.Precision.HIGHEST)
    cross_terms = lax.dot_general(weighted, mismatch, contract, precision=lax.Precision.HIGHEST)
    relative = mismatch / scale_rows[:, None]
    misfit_rows = live_mask * jnp.sqrt(jnp.mean(relative * relative, axis=1) + epsilon)
    return (gram_matrix, cross_terms, misfit_rows)


def solve_weights(gram_matrix, cross_terms):
    members = gram_matrix.shape[0]
    factor = jnp.linalg.cholesky(gram_matrix + inflation * jnp.eye(members, dtype=jnp.float32))
    return jax.scipy.linalg.cho_solve((factor, True), cross_terms)


def update_state(block, update_weights):
    state = block.astype(jnp.float32)
    members = state.shape[0]
    anomaly = (state - jnp.mean(state, axis=0, keepdims=True)) / math.sqrt(members - 1)
    moved = state + lax.dot_general(
        update_weights, anomaly, (((0,), (0,)), ((), ())), precision=lax.Precision.HIGHEST
    )
    return moved.astype(jnp.bfloat16)


def body(amplitude_maps, kept_blocks, block_owner, observed, error_scale, perturbation, model_slab):
    members, rows_here, map_width = amplitude_maps.shape
    devices = lax.axis_size("map")
    map_height = rows_here * devices
    table_w = dct_table(map_width)
    table_h = dct_table(map_height)
    rowwise = jnp.einsum(
        "ehw,kw->hke", amplitude_maps, table_w, preferred_element_type=jnp.float32
    ).astype(jnp.bfloat16)
    coefficients = jnp.einsum(
        "kh,hwe->wke",
        table_h,
        lax.all_to_all(rowwise, "map", split_axis=1, concat_axis=0, tiled=True),
        preferred_element_type=jnp.float32,
    ).astype(jnp.bfloat16)
    block_rows = coefficients.reshape(-1, BLK * members)
    candidates = block_rows.shape[0]
    keep_count = kept_blocks.shape[0]
    slot_count = devices * CAP
    dest_owner = block_owner[:, 0]
    positions = jnp.arange(keep_count, dtype=jnp.int32)
    earlier = (dest_owner[:, None] == dest_owner[None, :]) & (
        positions[None, :] < positions[:, None]
    )
    slot_rank = jnp.sum(earlier.astype(jnp.int32), axis=1)
    slot_index = dest_owner * CAP + slot_rank
    pick_slot = (slot_index[:, None] == jnp.arange(slot_count, dtype=jnp.int32)[None, :]).astype(
        jnp.bfloat16
    )
    weight_scale = members / (devices * keep_count * BLK)
    contract = (((0,), (0,)), ((), ()))
    pick_block = (kept_blocks[:, None] == jnp.arange(candidates, dtype=jnp.int32)[None, :]).astype(
        jnp.bfloat16
    )
    routing = lax.dot_general(
        pick_slot, pick_block, contract, preferred_element_type=jnp.float32
    ).astype(jnp.bfloat16)
    outgoing = jnp.dot(routing, block_rows, preferred_element_type=jnp.float32).astype(jnp.bfloat16)
    live_slots = jnp.sum(pick_slot.astype(jnp.float32), axis=0).astype(jnp.bfloat16)
    arrived, arrived_live = (
        lax.all_to_all(
            outgoing.reshape(devices, CAP, BLK * members),
            "map",
            split_axis=0,
            concat_axis=0,
            tiled=True,
        ),
        lax.all_to_all(
            live_slots.reshape(devices, CAP), "map", split_axis=0, concat_axis=0, tiled=True
        ),
    )
    predicted = arrived.reshape(-1, members).astype(jnp.float32)
    live_mask = jnp.repeat(arrived_live.astype(jnp.float32).reshape(-1), BLK)
    gram_matrix, cross_terms, data_misfit = gram_terms(
        predicted,
        observed.astype(jnp.float32),
        error_scale.astype(jnp.float32),
        perturbation.astype(jnp.float32),
        live_mask,
        weight_scale,
    )
    gram_matrix, cross_terms = lax.psum((gram_matrix, cross_terms), "map")
    update_weights = solve_weights(gram_matrix, cross_terms)
    updated_slab = update_state(model_slab, update_weights)
    return (updated_slab, update_weights, data_misfit)


def solution(mesh):
    in_specs = (
        P("groups", "map", None),
        P(("groups", "map")),
        P(("groups", "map"), None),
        P(("groups", "map")),
        P(("groups", "map")),
        P(("groups", "map"), None),
        P(None, ("groups", "map")),
    )
    out_specs = (P(None, ("groups", "map")), P("groups", None), P(("groups", "map")))
    return jax.shard_map(body, mesh=mesh, in_specs=in_specs, out_specs=out_specs, check_vma=False)
```

profile of v0, /device:TPU:0, one launch (start us, length us, event | category | flops | bytes accessed | tf_op | source)
XLA Modules:
  0.0 518.3 jit_solution(12664776586817616321)
XLA Ops:
  7.2 23.2 %fusion.9 = bf16[32,512,200]{1,2,0:T(8,128)(2,1)} fusion(bf16[200,32,512]{2,1,0:T(8,128)(2,1)} %param.7, f32[512]{0:T(512)S(1)} %get-tuple-element.50, f32[512]{0:T(512)S(1)} %get-tuple-element.49), kind=kOutput, calls=%fused_computation.10 | convolution fusion | flops 3359768576 | bytes 13111296 | tf_op jit(solution)/shard_map/ehw,kw->hke/dot_general | solution.py:63
  30.4 14.2 %copy.36 = bf16[32,512,200]{2,0,1:T(8,128)(2,1)} copy(bf16[32,512,200]{1,2,0:T(8,128)(2,1)} %fusion.9) | data formatting | bytes 13107200 | tf_op jit(solution)/shard_map/convert_element_type | solution.py:65
  44.6 7.5 %all-to-all-start = ((bf16[32,512,200]{2,0,1:T(8,128)(2,1)}), bf16[32,512,200]{2,0,1:T(8,128)(2,1)}, u32[]{:S(2)}, u32[]{:S(2)}) async-start(bf16[32,512,200]{2,0,1:T(8,128)(2,1)} %copy.36), calls=%async_computation | async-start | bytes 16777216 | tf_op jit(solution)/shard_map/all_to_all | solution.py:69
  53.2 3.2 convert_reduce_fusion
  56.4 146.5 %all-to-all-done = bf16[32,512,200]{2,0,1:T(8,128)(2,1)} async-done(((bf16[32,512,200]{2,0,1:T(8,128)(2,1)}), bf16[32,512,200]{2,0,1:T(8,128)(2,1)}, u32[]{:S(2)}, u32[]{:S(2)}) %all-to-all-start) | async-done | bytes 6553632 | tf_op jit(solution)/shard_map/all_to_all | solution.py:69
  202.9 51.4 %all-to-all-start.2 = ((bf16[16,1,2]{2,1,0:T(2,128)(2,1)}), bf16[16,1,2]{2,1,0:T(2,128)(2,1)S(1)}, u32[]{:S(2)}, u32[]{:S(2)}) async-start(bf16[16,1,2]{2,1,0:T(2,128)(2,1)} %all_to_all.29), calls=%async_computation.2 | async-start | bytes 16384 | tf_op jit(solution)/shard_map/all_to_all | solution.py:104
  254.3 12.3 %copy.38 = bf16[16,32,32,200]{3,2,1,0:T(8,128)(2,1)} copy(bf16[16,32,32,200]{3,1,2,0:T(8,128)(2,1)} %bitcast.7) | data formatting | bytes 13107200 | tf_op jit(solution)/shard_map/all_to_all | solution.py:69
  266.6 36.1 %fusion.12 = bf16[32,512,200]{1,2,0:T(8,128)(2,1)} fusion(bf16[512,32,200]{2,1,0:T(8,128)(2,1)} %bitcast.56, f32[512]{0:T(512)S(1)} %get-tuple-element.50, f32[512]{0:T(512)S(1)} %get-tuple-element.49), kind=kOutput, calls=%fused_computation.11 | convolution fusion | flops 3359768576 | bytes 13111296 | tf_op jit(solution)/shard_map/kh,hwe->wke/dot_general | solution.py:66
  302.6 10.6 %copy.40 = bf16[32,512,200]{2,1,0:T(8,128)(2,1)} copy(bf16[32,512,200]{1,2,0:T(8,128)(2,1)} %fusion.12) | data formatting | bytes 13107200 | tf_op jit(solution)/shard_map/convert_element_type | solution.py:71
  313.3 14.8 %reshape.103 = bf16[2048,1600]{1,0:T(8,128)(2,1)} reshape(bf16[32,512,200]{2,1,0:T(8,128)(2,1)} %copy.40) | data formatting | bytes 13107200 | tf_op jit(solution)/shard_map/reshape | solution.py:72
  328.1 4.4 convolution_convert_fusion.1
  333.2 6.1 %all-to-all-start.1 = ((bf16[16,2,1600]{2,1,0:T(2,128)(2,1)}), bf16[16,2,1600]{2,1,0:T(2,128)(2,1)S(1)}, u32[]{:S(2)}, u32[]{:S(2)}) async-start(bf16[16,2,1600]{2,1,0:T(2,128)(2,1)} %reshape.104), calls=%async_computation.1 | async-start | bytes 212992 | tf_op jit(solution)/shard_map/all_to_all | solution.py:97
  339.9 7.0 %all-to-all-done.1 = bf16[16,2,1600]{2,1,0:T(2,128)(2,1)S(1)} async-done(((bf16[16,2,1600]{2,1,0:T(2,128)(2,1)}), bf16[16,2,1600]{2,1,0:T(2,128)(2,1)S(1)}, u32[]{:S(2)}, u32[]{:S(2)}) %all-to-all-start.1) | async-done | bytes 102432 | tf_op jit(solution)/shard_map/all_to_all | solution.py:97
  348.2 1.4 fusion.26
  351.3 1.3 fusion.58
  352.6 86.8 %all-reduce.6.cloned.1.call-done = (f32[200,200]{1,0:T(8,128)}, f32[200,200]{1,0:T(8,128)}) async-done(((f32[200,200]{1,0:T(8,128)}, f32[200,200]{1,0:T(8,128)}), (f32[200,200]{1,0:T(8,128)}, f32[200,200]{1,0:T(8,128)})) %all-reduce.6.cloned.1.call-update) | async-done | bytes 320016 | tf_op jit(solution)/shard_map/psum | solution.py:118
  440.5 1.0 fusion.29
  441.4 11.7 %cholesky.50 = f32[128,128]{1,0:T(8,128)S(1)} custom-call(f32[128,128]{1,0:T(8,128)S(1)} %cholesky.121), custom_call_target="Cholesky" | custom-call | tf_op jit(solution)/shard_map/jit(cholesky)/cholesky | solution.py:43
  453.2 9.8 %custom-call.18 = f32[1,128,128]{1,2,0:T(8,128)S(1)} custom-call(f32[1,128,128]{2,1,0:T(8,128)S(1)} %get-tuple-element.42), custom_call_target="InvertDiagBlocksLowerTriangular" | custom-call | tf_op jit(solution)/shard_map/jit(cholesky)/cholesky | solution.py:43
  463.5 6.6 %cholesky.108 = f32[72,72]{1,0:T(8,128)S(1)} custom-call(f32[72,72]{1,0:T(8,128)S(1)} %convolution_subtract_fusion.2), custom_call_target="Cholesky" | custom-call | tf_op jit(solution)/shard_map/jit(cholesky)/cholesky | solution.py:43
  472.8 19.8 %custom-call.19 = f32[2,128,128]{1,2,0:T(8,128)S(1)} custom-call(f32[2,128,128]{2,1,0:T(8,128)S(1)} %pad_maximum_fusion.1), custom_call_target="InvertDiagBlocksLowerTriangular" | custom-call | tf_op jit(solution)/shard_map/jit(_cho_solve)/triangular_solve | solution.py:44
  492.7 1.3 fusion.30
  494.0 1.2 convolution_subtract_fusion.1
  497.3 13.9 %fusion = bf16[200,12288]{1,0:T(8,128)(2,1)} fusion(bf16[200,12288]{1,0:T(8,128)(2,1)} %param.13, f32[12288]{0:T(1024)S(1)} %broadcast_multiply_fusion.1, f32[72,200]{0,1:T(8,128)S(1)} %copy.44, f32[128,200]{0,1:T(8,128)S(1)} %fusion.41), kind=kOutput, calls=%fused_computation.1 | convolution fusion | flops 5913025536 | bytes 10039552 | tf_op jit(solution)/shard_map/dot_general | solution.py:51
  (65 shorter events, 10.1 us)
Async XLA Ops:
  44.6 7.6 %copy-start.3 = (s32[16,1]{0,1:T(1,128)S(1)}, s32[16,1]{0,1:T(1,128)}, u32[]{:S(2)}) copy-start(s32[16,1]{0,1:T(1,128)} %param.9) | copy-start | bytes 196
  44.6 158.3 %all-to-all-start = ((bf16[32,512,200]{2,0,1:T(8,128)(2,1)}), bf16[32,512,200]{2,0,1:T(8,128)(2,1)}, u32[]{:S(2)}, u32[]{:S(2)}) async-start(bf16[32,512,200]{2,0,1:T(8,128)(2,1)} %copy.36), calls=%async_computation | async-start | bytes 16777216 | tf_op jit(solution)/shard_map/all_to_all | solution.py:69
  202.9 130.4 %all-to-all-start.2 = ((bf16[16,1,2]{2,1,0:T(2,128)(2,1)}), bf16[16,1,2]{2,1,0:T(2,128)(2,1)S(1)}, u32[]{:S(2)}, u32[]{:S(2)}) async-start(bf16[16,1,2]{2,1,0:T(2,128)(2,1)} %all_to_all.29), calls=%async_computation.2 | async-start | bytes 16384 | tf_op jit(solution)/shard_map/all_to_all | solution.py:104
  313.3 14.9 %copy-start.1 = (s32[16]{0:T(128)S(1)}, s32[16]{0:T(128)}, u32[]{:S(2)}) copy-start(s32[16]{0:T(128)} %param.8) | copy-start | bytes 196
  313.3 26.2 %copy-start.2 = (bf16[256]{0:T(256)(128)(2,1)S(1)}, bf16[256]{0:T(256)(128)(2,1)}, u32[]{:S(2)}) copy-start(bf16[256]{0:T(256)(128)(2,1)} %param.11) | copy-start | bytes 1540
  313.3 26.2 %copy-start = (bf16[256,200]{0,1:T(8,128)(2,1)S(1)}, bf16[256,200]{0,1:T(8,128)(2,1)}, u32[]{:S(2)}) copy-start(bf16[256,200]{0,1:T(8,128)(2,1)} %param.12) | copy-start | bytes 307204
  313.3 26.3 %copy-start.4 = (bf16[256]{0:T(256)(128)(2,1)S(1)}, bf16[256]{0:T(256)(128)(2,1)}, u32[]{:S(2)}) copy-start(bf16[256]{0:T(256)(128)(2,1)} %param.10) | copy-start | bytes 1540
  333.2 13.7 %all-to-all-start.1 = ((bf16[16,2,1600]{2,1,0:T(2,128)(2,1)}), bf16[16,2,1600]{2,1,0:T(2,128)(2,1)S(1)}, u32[]{:S(2)}, u32[]{:S(2)}) async-start(bf16[16,2,1600]{2,1,0:T(2,128)(2,1)} %reshape.104), calls=%async_computation.1 | async-start | bytes 212992 | tf_op jit(solution)/shard_map/all_to_all | solution.py:97
  339.4 100.0 %all-reduce.6.cloned.1.call-start = ((), (), s32[]{:S(2)}) async-start(), calls=%async_computation.3 | async-start | bytes 819200 | tf_op jit(solution)/shard_map/psum | solution.py:118
Sparse Core Ops, SparseCore 0:
  352.7 86.6 all-reduce.5
where the time goes:
time: 521 us; the launch traced here: 518 us
  waiting for transfers between devices  240 us (46%)
  matrix products  84.4 us (16%)
  starting transfers between devices  65 us (12%)
  local copies, waits for them, and re-layouts  56.6 us (11%)
  other arithmetic  56 us (11%)
  between operations  15.9 us (3%)
    all_to_all x1, waiting for transfers between devices, body(): lax.all_to_all(rowwise, 'map', split_axis=1, concat_axis=0, tiled=True)  147 us
    psum x1, waiting for transfers between devices, body(): gram_matrix, cross_terms = lax.psum((gram_matrix, cross_terms), 'map')  86.8 us
    all_to_all x1, starting transfers between devices, body(): lax.all_to_all(live_slots.reshape(devices, CAP), 'map', split_axis=0, con...  51.4 us
    dot_general x1, matrix products, body(): jnp.einsum('kh,hwe->wke', table_h, lax.all_to_all(rowwise, 'map', split_a...  36.1 us
    another operation x7, other arithmetic, solve_weights(): jnp.linalg.cholesky(gram_matrix + inflation * jnp.eye(members, dtype=jnp....  29.4 us
    dot_general x1, matrix products, body(): jnp.einsum('ehw,kw->hke', amplitude_maps, table_w, preferred_element_type...  23.2 us
    another operation x7, other arithmetic, solve_weights(): return jax.scipy.linalg.cho_solve((factor, True), cross_terms)  20 us
    reshape x1, local copies, waits for them, and re-layouts, body(): block_rows = coefficients.reshape(-1, BLK * members)  14.8 us
  transfers between devices with their start and end apart: 4, of which 3 were waited for; matrix products, arithmetic and copies ran while one was open for 16% of the time, Pallas kernels for 0%

commit v1 on v0

--- a/solution.py
+++ b/solution.py
@@ -1,16 +1,23 @@
+import functools
 import math
 
 import jax
 import jax.numpy as jnp
+import numpy as np
 from jax import lax
+from jax.experimental import pallas as pl
+from jax.experimental.pallas import tpu as pltpu
 from jax.sharding import PartitionSpec as P
 
 BLK = 8
 CAP = 2
+LANES = 128
 
 
 inflation = 4.0
 epsilon = 1e-06
+MESH = pl.DeviceIdType.MESH
+VMEM = pltpu.VMEM
 
 
 def dct_table(length):
@@ -18,6 +25,16 @@
     sample = jnp.arange(length, dtype=jnp.float32)[None, :]
     cosine_table = jnp.cos(math.pi * (2.0 * sample + 1.0) * frequency / (2.0 * length))
     factor = jnp.where(frequency == 0, math.sqrt(1.0 / length), math.sqrt(2.0 / length))
+    return (cosine_table * factor).astype(jnp.bfloat16)
+
+
+def dct_constant(length):
+    f32 = np.float32
+    frequency = np.arange(length, dtype=f32)[:, None]
+    sample = np.arange(length, dtype=f32)[None, :]
+    angle = f32(math.pi) * (f32(2) * sample + f32(1)) * frequency / f32(2 * length)
+    cosine_table = np.cos(angle.astype(np.float64)).astype(f32)
+    factor = np.where(frequency == 0, f32(math.sqrt(1.0 / length)), f32(math.sqrt(2.0 / length)))
     return (cosine_table * factor).astype(jnp.bfloat16)
 
 
@@ -54,7 +71,7 @@
     return moved.astype(jnp.bfloat16)
 
 
-def body(amplitude_maps, kept_blocks, block_owner, observed, error_scale, perturbation, model_slab):
+def body_large(amplitude_maps, kept_blocks, block_owner, observed, error_scale, perturbation, model_slab):
     members, rows_here, map_width = amplitude_maps.shape
     devices = lax.axis_size("map")
     map_height = rows_here * devices
@@ -121,6 +138,331 @@
     return (updated_slab, update_weights, data_misfit)
 
 
+def transform_kernel(rows_here, maps_ref, row_table_ref, column_table_ref, part_ref, rowwise_ref):
+    chunk, _, width = maps_ref.shape
+    flat = maps_ref[...].reshape(chunk * rows_here, width)
+    rowwise = lax.dot_general(
+        flat, row_table_ref[...], (((1,), (1,)), ((), ())), preferred_element_type=jnp.float32
+    )
+    halves = rowwise_ref.shape[0]
+    for half in range(halves):
+        rowwise_ref[half] = rowwise[:, half * LANES : (half + 1) * LANES]
+
+    def tile(t, carry):
+        for half in range(halves):
+            lanes = slice(half * LANES, (half + 1) * LANES)
+            total = [None] * BLK
+            for h in range(rows_here):
+                row = rowwise_ref[half, pl.ds(t * 8 * rows_here + h, 8, stride=rows_here), :]
+                row = row.astype(jnp.bfloat16).astype(jnp.float32)
+                for c in range(BLK):
+                    term = row * column_table_ref[h, c : c + 1, lanes]
+                    total[c] = term if total[c] is None else total[c] + term
+            for c in range(BLK):
+                part_ref[c * halves + half, pl.ds(pl.multiple_of(t * 8, 8), 8), :] = total[c]
+        return carry
+
+    lax.fori_loop(0, chunk // 8, tile, 0)
+
+
+def transform(maps, row_table, column_table):
+    members, rows_here, width = maps.shape
+    blocks = row_table.shape[0]
+    chunk = 40
+    pieces = BLK * blocks // LANES
+    return pl.pallas_call(
+        functools.partial(transform_kernel, rows_here),
+        grid=(members // chunk,),
+        out_shape=jax.ShapeDtypeStruct((pieces, members, LANES), jnp.float32),
+        in_specs=[
+            pl.BlockSpec((chunk, rows_here, width), lambda i: (i, 0, 0)),
+            pl.BlockSpec((blocks, width), lambda i: (0, 0)),
+            pl.BlockSpec((rows_here, BLK, blocks), lambda i: (0, 0, 0)),
+        ],
+        out_specs=pl.BlockSpec((pieces, chunk, LANES), lambda i: (0, i, 0)),
+        scratch_shapes=[VMEM((blocks // LANES, chunk * rows_here, LANES), jnp.float32)],
+        compiler_params=pltpu.CompilerParams(vmem_limit_bytes=40 * 2**20),
+        name="transform",
+    )(maps, row_table, column_table)
+
+
+def combine_kernel(
+    part_ref, out_ref, held, from_core, from_x, from_z, sends, recvs
+):
+    members = part_ref.shape[1]
+    me = lax.axis_index("map")
+    core = lax.rem(me, 2)
+    x = lax.rem(me // 2, 2)
+    z = me // 4
+    core_peer = me + 1 - 2 * core
+    x_peer = me + 2 - 4 * x
+    z_peers = [lax.rem(z + s, 4) * 4 + x * 2 + core for s in (1, 2, 3)]
+
+    barrier = pltpu.get_barrier_semaphore()
+    for peer in [core_peer, x_peer] + z_peers:
+        pl.semaphore_signal(barrier, inc=1, device_id={"map": peer}, device_id_type=MESH)
+    pl.semaphore_wait(barrier, 5)
+
+    def send(number, src, dst, peer):
+        copy = pltpu.make_async_remote_copy(
+            src_ref=src,
+            dst_ref=dst,
+            send_sem=sends.at[number],
+            recv_sem=recvs.at[number],
+            device_id={"map": peer},
+            device_id_type=MESH,
+        )
+        copy.start()
+        return copy
+
+    first = []
+    for xi in range(2):
+        xx = 1 - x if xi == 0 else x
+        for zi in range(4):
+            n = xi * 4 + zi
+            first.append(
+                send(n, part_ref.at[zi * 4 + xx * 2 + 1 - core], from_core.at[n], core_peer)
+            )
+    second = []
+    for n in range(4):
+        first[n].wait_recv()
+        held[n] = part_ref[n * 4 + (1 - x) * 2 + core] + from_core[n]
+        second.append(send(8 + n, held.at[n], from_x.at[n], x_peer))
+    third = []
+    for s in (1, 2, 3, 0):
+        zi = lax.rem(z + s, 4)
+        if s == 1:
+            for n in range(4):
+                first[4 + n].wait_recv()
+                second[n].wait_recv()
+        held[4 + s] = part_ref[zi * 4 + x * 2 + core] + from_core[4 + zi] + from_x[zi]
+        if s:
+            third.append(send(12 + s - 1, held.at[4 + s], from_z.at[s - 1], z_peers[s - 1]))
+    for copy in third:
+        copy.wait_recv()
+    total = held[4] + from_z[0] + from_z[1] + from_z[2]
+    pad = out_ref.shape[1] - members
+    mine = jnp.concatenate([total, jnp.zeros((pad, LANES), jnp.float32)], axis=0)
+    out_ref[me] = mine.astype(jnp.bfloat16)
+
+    fourth = [send(15 + s, out_ref.at[me], out_ref.at[me], z_peers[s]) for s in range(3)]
+    fifth = [send(18, out_ref.at[me], out_ref.at[me], x_peer)]
+    sixth = [send(22, out_ref.at[me], out_ref.at[me], core_peer)]
+    for s in range(3):
+        fourth[s].wait_recv()
+        piece = lax.rem(z + 3 - s, 4) * 4 + x * 2 + core
+        fifth.append(send(19 + s, out_ref.at[piece], out_ref.at[piece], x_peer))
+        sixth.append(send(23 + s, out_ref.at[piece], out_ref.at[piece], core_peer))
+    for n in range(4):
+        fifth[n].wait_recv()
+        piece = lax.rem(z + 4 - n, 4) * 4 + (1 - x) * 2 + core
+        sixth.append(send(26 + n, out_ref.at[piece], out_ref.at[piece], core_peer))
+    for copy in sixth:
+        copy.wait_recv()
+    for copy in first + second + third + fourth + fifth + sixth:
+        copy.wait_send()
+
+
+def combine(parts):
+    pieces, members, _ = parts.shape
+    padded = -(-members // 16) * 16
+    piece = (members, LANES)
+    return pl.pallas_call(
+        combine_kernel,
+        out_shape=jax.ShapeDtypeStruct((pieces, padded, LANES), jnp.bfloat16),
+        in_specs=[pl.BlockSpec(memory_space=VMEM)],
+        out_specs=pl.BlockSpec(memory_space=VMEM),
+        scratch_shapes=[
+            VMEM((8,) + piece, jnp.float32),
+            VMEM((8,) + piece, jnp.float32),
+            VMEM((4,) + piece, jnp.float32),
+            VMEM((3,) + piece, jnp.float32),
+            pltpu.SemaphoreType.DMA((30,)),
+            pltpu.SemaphoreType.DMA((30,)),
+        ],
+        compiler_params=pltpu.CompilerParams(
+            collective_id=0, has_side_effects=True, vmem_limit_bytes=40 * 2**20
+        ),
+        name="combine",
+    )(parts)
+
+
+def solve_kernel(
+    weight_scale, predicted_ref, data_ref, weights_ref, high_ref, low_ref, misfit_ref,
+    weighted, paired, system,
+):
+    pieces = predicted_ref.shape[0]
+    members = weights_ref.shape[0]
+    halves = data_ref.shape[2] // LANES
+    wide = 256
+    for n in range(pieces):
+        c, half = divmod(n, halves)
+        lanes = slice(half * LANES, (half + 1) * LANES)
+        here = slice(n * LANES, (n + 1) * LANES)
+        predicted = predicted_ref[n].astype(jnp.float32)[:members]
+        data = data_ref[c, :, lanes].astype(jnp.float32)
+        noise = data[:members]
+        observed = data[members : members + 1]
+        scale = data[members + 1 : members + 2]
+        center = jnp.sum(predicted, axis=0, keepdims=True) / members
+        anomaly = (predicted - center) / math.sqrt(members - 1)
+        weight = weight_scale / (scale * scale)
+        mismatch = observed + math.sqrt(inflation) * scale * noise - predicted
+        relative = mismatch / scale
+        misfit_ref[c : c + 1, lanes] = jnp.sqrt(
+            jnp.sum(relative * relative, axis=0, keepdims=True) / members + epsilon
+        )
+        weighted[:, here] = anomaly * weight
+        paired[0:members, here] = anomaly
+        paired[wide : wide + members, here] = mismatch
+    contract = (((1,), (1,)), ((), ()))
+    for part in range(2):
+        rows = slice(part * wide, part * wide + members)
+        product = lax.dot_general(
+            weighted[...], paired[rows, :], contract,
+            preferred_element_type=jnp.float32, precision=lax.Precision.HIGHEST,
+        )
+        if part == 0:
+            i = lax.broadcasted_iota(jnp.int32, product.shape, 0)
+            j = lax.broadcasted_iota(jnp.int32, product.shape, 1)
+            product = product + jnp.where(i == j, inflation, 0.0)
+        system[:, part * wide : part * wide + members] = product
+    width = system.shape[1]
+    sub = lax.broadcasted_iota(jnp.int32, (8, 1), 0)
+    row_number = lax.broadcasted_iota(jnp.int32, (members, 1), 0)
+    for k in range(members // 8):
+        start = 8 * k
+        low = start // LANES * LANES
+        block = system[start : start + 8, low:width]
+        for j in range(8):
+            at = start - low + j
+            column = block[:, at : at + 1]
+            pivot = block[j : j + 1, :] / column[j : j + 1, :]
+            block = jnp.where(sub == j, pivot, block - column * pivot)
+        columns = system[:, start : start + 8]
+        outside = (row_number < start) | (row_number >= start + 8)
+        columns = jnp.where(outside, columns, 0.0)
+        system[:, low:width] = system[:, low:width] - jnp.dot(
+            columns, block, preferred_element_type=jnp.float32, precision=lax.Precision.HIGHEST
+        )
+        system[start : start + 8, low:width] = block
+    solved = system[:, wide : wide + members]
+    weights_ref[...] = solved
+    centred = (solved - jnp.sum(solved, axis=0, keepdims=True) / members) / math.sqrt(members - 1)
+    turned = centred.T
+    high = turned.astype(jnp.bfloat16)
+    high_ref[...] = high
+    low_ref[...] = (turned - high.astype(jnp.float32)).astype(jnp.bfloat16)
+
+
+def solve(predicted, data, members, weight_scale):
+    pieces = predicted.shape[0]
+    cells = pieces * LANES
+    square = (members, members)
+    return pl.pallas_call(
+        functools.partial(solve_kernel, weight_scale),
+        out_shape=(
+            jax.ShapeDtypeStruct(square, jnp.float32),
+            jax.ShapeDtypeStruct(square, jnp.bfloat16),
+            jax.ShapeDtypeStruct(square, jnp.bfloat16),
+            jax.ShapeDtypeStruct((data.shape[0], data.shape[2]), jnp.float32),
+        ),
+        in_specs=[pl.BlockSpec(memory_space=VMEM)] * 2,
+        out_specs=(pl.BlockSpec(memory_space=VMEM),) * 4,
+        scratch_shapes=[
+            VMEM((members, cells), jnp.float32),
+            VMEM((256 + members, cells), jnp.float32),
+            VMEM((members, 512), jnp.float32),
+        ],
+        compiler_params=pltpu.CompilerParams(vmem_limit_bytes=40 * 2**20),
+        name="solve",
+    )(predicted, data)
+
+
+def update_kernel(high_ref, low_ref, slab_ref, out_ref):
+    state = slab_ref[...]
+    moved = jnp.dot(high_ref[...], state, preferred_element_type=jnp.float32)
+    moved = moved + jnp.dot(low_ref[...], state, preferred_element_type=jnp.float32)
+    out_ref[...] = (state.astype(jnp.float32) + moved).astype(jnp.bfloat16)
+
+
+def update(high, low, slab):
+    members, cells = slab.shape
+    tile = 1024
+    whole = pl.BlockSpec((members, members), lambda i: (0, 0))
+    column = pl.BlockSpec((members, tile), lambda i: (0, i))
+    return pl.pallas_call(
+        update_kernel,
+        grid=(cells // tile,),
+        out_shape=jax.ShapeDtypeStruct(slab.shape, jnp.bfloat16),
+        in_specs=[whole, whole, column],
+        out_specs=column,
+        compiler_params=pltpu.CompilerParams(vmem_limit_bytes=40 * 2**20),
+        name="update",
+    )(high, low, slab)
+
+
+def body_small(amplitude_maps, kept_blocks, block_owner, observed, error_scale, perturbation, model_slab):
+    members, rows_here, map_width = amplitude_maps.shape
+    devices = lax.axis_size("map")
+    me = lax.axis_index("map")
+    map_height = rows_here * devices
+    keep_count = kept_blocks.shape[0]
+    columns_here = map_width // devices
+    per_column = map_height // BLK
+    table_w = jnp.asarray(dct_constant(map_width))
+    table_h = jnp.asarray(dct_constant(map_height))
+
+    names = jnp.stack([kept_blocks, block_owner[:, 0]])
+    names = lax.all_gather(names, "map")
+    local = jnp.concatenate(
+        [perturbation, observed[:, None], error_scale[:, None]], axis=1
+    )
+    local = lax.all_gather(local, "map", tiled=True)
+
+    blocks = names[:, 0, :].reshape(-1)
+    owners = names[:, 1, :]
+    source = jnp.repeat(jnp.arange(devices, dtype=jnp.int32), keep_count)
+    column_of = source * columns_here + blocks // per_column
+    row_of = blocks % per_column
+    one = jnp.bfloat16
+    pick_column = (column_of[:, None] == jnp.arange(map_width, dtype=jnp.int32)[None, :]).astype(one)
+    row_table = jnp.dot(pick_column, table_w, preferred_element_type=jnp.float32).astype(one)
+    pick_row = (row_of[:, None] == jnp.arange(per_column, dtype=jnp.int32)[None, :]).astype(one)
+    here = lax.dynamic_slice_in_dim(table_h, me * rows_here, rows_here, axis=1)
+    column_table = jnp.einsum(
+        "bk,kch->hcb",
+        pick_row,
+        here.reshape(per_column, BLK, rows_here),
+        preferred_element_type=jnp.float32,
+    )
+    parts = transform(amplitude_maps, row_table, column_table)
+    predicted = combine(parts)
+
+    positions = jnp.arange(keep_count, dtype=jnp.int32)
+    earlier = (owners[:, :, None] == owners[:, None, :]) & (
+        positions[None, None, :] < positions[None, :, None]
+    )
+    rank = jnp.sum(earlier.astype(jnp.int32), axis=2)
+    slot = ((owners * devices + jnp.arange(devices, dtype=jnp.int32)[:, None]) * CAP + rank).reshape(-1)
+    slots = devices * devices * CAP
+    pick_slot = (jnp.arange(slots, dtype=jnp.int32)[:, None] == slot[None, :]).astype(one)
+    data = jnp.einsum(
+        "sce,sb->ceb",
+        local.reshape(slots, BLK, members + 2),
+        pick_slot,
+        preferred_element_type=jnp.float32,
+    ).astype(one)
+    weight_scale = members / (devices * keep_count * BLK)
+    update_weights, high, low, misfit = solve(predicted, data, members, weight_scale)
+    updated_slab = update(high, low, model_slab)
+    mine = lax.dynamic_slice_in_dim(pick_slot, me * devices * CAP, devices * CAP, axis=0)
+    data_misfit = jnp.einsum(
+        "sb,cb->sc", mine.astype(jnp.float32), misfit, precision=lax.Precision.HIGHEST
+    ).reshape(-1)
+    return (updated_slab, update_weights, data_misfit)
+
+
 def solution(mesh):
     in_specs = (
         P("groups", "map", None),
@@ -132,4 +474,12 @@
         P(None, ("groups", "map")),
     )
     out_specs = (P(None, ("groups", "map")), P("groups", None), P(("groups", "map")))
-    return jax.shard_map(body, mesh=mesh, in_specs=in_specs, out_specs=out_specs, check_vma=False)
+    devices = mesh.shape["map"]
+
+    def run(*args):
+        kept = args[1].shape[0] // mesh.shape["groups"]
+        fits = devices == 16 and kept * BLK == devices * LANES
+        body = body_small if fits else body_large
+        return jax.shard_map(body, mesh=mesh, in_specs=in_specs, out_specs=out_specs, check_vma=False)(*args)
+
+    return run

time: 521 us -> 138 us (0.26)
  waiting for transfers between devices: 240 us -> 0.04 us
  Pallas kernels: 0 us -> 82.7 us
  matrix products: 84.4 us -> 2.88 us
  starting transfers between devices: 65 us -> 0.04 us
  other arithmetic: 56 us -> 2.82 us
  local copies, waits for them, and re-layouts: 56.6 us -> 12.1 us
  blocking collectives: 0 us -> 23.1 us
    all_to_all x3 -> x0, waiting for transfers between devices: 154 us -> none  [the longest x1 147 us: body(): lax.all_to_all(rowwise, 'map', split_axis=1, concat_axis=0, tiled=True)]
    psum x1 -> x0, waiting for transfers between devices: 86.8 us -> none  [body(): gram_matrix, cross_terms = lax.psum((gram_matrix, cross_terms), 'map')]
    pallas_call x0 -> x4, Pallas kernels: none -> 82.7 us  [the longest x1 34.6 us: combine(): pl.pallas_call(combine_kernel, out_shape=jax.ShapeDtypeStruct((pieces, pa...]
    dot_general x6 -> x4, matrix products: 80.3 us -> 2.88 us  [the longest x1 1.39 us: body_small(): jnp.dot(pick_column, table_w, preferred_element_type=jnp.float32)]
    all_to_all x3 -> x0, starting transfers between devices: 65 us -> none  [the longest x1 51.4 us: body(): lax.all_to_all(live_slots.reshape(devices, CAP), 'map', split_axis=0, con...]
    another operation x14 -> x0, other arithmetic: 49.4 us -> none  [the longest x7 29.4 us: solve_weights(): jnp.linalg.cholesky(gram_matrix + inflation * jnp.eye(members, dtype=jnp....]
    convert_element_type x4 -> x0, local copies, waits for them, and re-layouts: 25.2 us -> none  [the longest x1 14.2 us: body(): rowwise = jnp.einsum('ehw,kw->hke', amplitude_maps, table_w, preferred_el...]
    all_gather x0 -> x1, blocking collectives: none -> 23.1 us  [body_small(): names = lax.all_gather(names, 'map')]
  transfers between devices with their start and end apart: 4 -> 1, of which waited for: 3 -> 0; matrix products, arithmetic and copies ran while one was open for 16% -> 3% of each run, Pallas kernels for 0% -> 33%
where the time goes in v1:
time: 138 us
  Pallas kernels  82.7 us (60%)
  blocking collectives  23.1 us (17%)
  between operations  14.1 us (10%)
  local copies, waits for them, and re-layouts  12.1 us (9%)
  matrix products  2.88 us (2%)
  other arithmetic  2.82 us (2%)
    pallas_call x1, Pallas kernels, combine(): pl.pallas_call(combine_kernel, out_shape=jax.ShapeDtypeStruct((pieces, pa...  34.6 us
    pallas_call x1, Pallas kernels, solve(): pl.pallas_call(functools.partial(solve_kernel, weight_scale), out_shape=(...  30.3 us
    all_gather x1, blocking collectives, body_small(): names = lax.all_gather(names, 'map')  23.1 us
    pallas_call x1, Pallas kernels, transform(): pl.pallas_call(functools.partial(transform_kernel, rows_here), grid=(memb...  10.4 us
    pallas_call x1, Pallas kernels, update(): pl.pallas_call(update_kernel, grid=(cells // tile,), out_shape=jax.ShapeD...  7.41 us
    unnamed x4, local copies, waits for them, and re-layouts  5.32 us
    all_gather x1, local copies, waits for them, and re-layouts, body_small(): local = lax.all_gather(local, 'map', tiled=True)  3.37 us
  transfers between devices with their start and end apart: 1, of which 0 were waited for; matrix products, arithmetic and copies ran while one was open for 3% of the time, Pallas kernels for 33%

profile of v1, /device:TPU:0, one launch (start us, length us, event | category | flops | bytes accessed | tf_op | source)
XLA Modules:
  0.0 137.9 jit_solution(4930836783973267142)
XLA Ops:
  7.2 0.7 broadcast_in_dim.9
  7.9 0.7 broadcast_in_dim.10
  8.5 1.5 %pad_maximum_fusion = bf16[256,202]{0,1:T(8,128)(2,1)} fusion(bf16[256,1]{0,1:T(2,128)(2,1)S(1)} %broadcast_in_dim.10, bf16[256,1]{0,1:T(2,128)(2,1)S(1)} %broadcast_in_dim.9, bf16[256,200]{0,1:T(8,128)(2,1)} %param.14), kind=kLoop, calls=%fused_computation.11 | loop fusion | flops 310272 | bytes 206848 | tf_op jit(solution)/shard_map/concatenate | solution.py:418
  10.1 0.1 reshape.111
  10.2 0.7 add_bitcast_fusion
  10.9 23.1 %all-gather.1 = s32[16,2,16]{2,1,0:T(2,128)S(1)} all-gather(s32[1,2,16]{2,1,0:T(2,128)S(1)} %add_bitcast_fusion), channel_id=2, replica_groups=mesh['groups'=2,'map'=16] {'map'}, dimensions={0}, use_global_device_ids=true | all-gather | bytes 2176 | tf_op jit(solution)/shard_map/all_gather | solution.py:417
  34.0 0.1 mul.43
  34.2 0.4 convert_reduce_fusion
  34.6 0.1 reduce_sum.12
  34.7 1.0 dynamic-slice_bitcast_fusion
  35.7 0.1 copy.22
  35.9 0.2 convolution_bitcast_fusion.column_table_ref
  36.1 1.4 %convolution_convert_fusion.row_table_ref = bf16[256,512]{1,0:T(8,128)(2,1)S(1)} fusion(bf16[512,512]{1,0:T(8,128)(2,1)} %constant.47.clone, s32[256]{0:T(256)S(1)} %get-tuple-element.15), kind=kOutput, calls=%fused_computation.3 | convolution fusion | flops 134479872 | bytes 787456 | tf_op jit(solution)/shard_map/dot_general | solution.py:430
  37.5 2.9 %copy-done = bf16[200,32,512]{2,1,0:T(8,128)(2,1)S(1)} copy-done((bf16[200,32,512]{2,1,0:T(8,128)(2,1)S(1)}, bf16[200,32,512]{2,1,0:T(8,128)(2,1)}, u32[]{:S(2)}) %copy-start) | copy-done | bytes 6553624
  40.4 10.4 %transform.1.part_ref = f32[16,200,128]{2,1,0:T(8,128)S(1)} custom-call(bf16[200,32,512]{2,1,0:T(8,128)(2,1)S(1)} %copy-done, bf16[256,512]{1,0:T(8,128)(2,1)S(1)} %convolution_convert_fusion.row_table_ref, f32[32,8,256]{2,1,0:T(8,128)S(1)} %convolution_bitcast_fusion.column_table_ref), custom_call_target="tpu_custom_call" | custom-call | tf_op jit(solution)/shard_map/transform/pallas_call | solution.py:173
  50.8 34.6 %combine.1.predicted_ref = bf16[16,208,128]{2,1,0:T(8,128)(2,1)S(1)} custom-call(f32[16,200,128]{2,1,0:T(8,128)S(1)} %transform.1.part_ref), custom_call_target="tpu_custom_call" | custom-call | tf_op jit(solution)/shard_map/combine/pallas_call | solution.py:270
  85.4 0.1 iota_compare_fusion
  85.5 3.4 %copy.23 = bf16[4096,202]{1,0:T(8,128)(2,1)S(1)} copy(bf16[4096,202]{0,1:T(8,128)(2,1)} %all-gather.4.cloned.1.call-done) | data formatting | bytes 3309568 | tf_op jit(solution)/shard_map/all_gather | solution.py:421
  88.9 1.2 fusion.2.data_ref
  90.1 30.3 %solve.1 = (f32[200,200]{1,0:T(8,128)}, bf16[200,200]{1,0:T(8,128)(2,1)S(1)}, bf16[200,200]{1,0:T(8,128)(2,1)S(1)}, f32[8,256]{1,0:T(8,128)S(1)}) custom-call(bf16[16,208,128]{2,1,0:T(8,128)(2,1)S(1)} %combine.1.predicted_ref, bf16[8,202,256]{2,1,0:T(8,128)(2,1)S(1)} %fusion.2.data_ref), custom_call_target="tpu_custom_call" | custom-call | tf_op jit(solution)/shard_map/solve/pallas_call | solution.py:362
  120.4 0.1 fusion.10
  120.6 0.7 reshape.114
  121.2 2.4 %copy-done.1 = bf16[200,12288]{1,0:T(8,128)(2,1)S(1)} copy-done((bf16[200,12288]{1,0:T(8,128)(2,1)S(1)}, bf16[200,12288]{1,0:T(8,128)(2,1)}, u32[]{:S(2)}) %copy-start.1) | copy-done | bytes 4915224
  123.6 7.4 %update.1 = bf16[200,12288]{1,0:T(8,128)(2,1)} custom-call(bf16[200,200]{1,0:T(8,128)(2,1)S(1)} %get-tuple-element.7.high_ref, bf16[200,200]{1,0:T(8,128)(2,1)S(1)} %get-tuple-element.8.low_ref, bf16[200,12288]{1,0:T(8,128)(2,1)S(1)} %copy-done.1), custom_call_target="tpu_custom_call" | custom-call | tf_op jit(solution)/shard_map/update/pallas_call | solution.py:394
  (10 shorter events, 0.2 us)
Async XLA Ops:
  7.2 78.4 %all-gather.4.cloned.1.call-start = ((), (), s32[]{:S(2)}) async-start(), calls=%async_computation | async-start | bytes 1810432 | tf_op jit(solution)/shard_map/all_gather | solution.py:421
  37.5 2.9 %copy-start = (bf16[200,32,512]{2,1,0:T(8,128)(2,1)S(1)}, bf16[200,32,512]{2,1,0:T(8,128)(2,1)}, u32[]{:S(2)}) copy-start(bf16[200,32,512]{2,1,0:T(8,128)(2,1)} %maps_ref.1) | copy-start | bytes 19660804
  121.2 2.4 %copy-start.1 = (bf16[200,12288]{1,0:T(8,128)(2,1)S(1)}, bf16[200,12288]{1,0:T(8,128)(2,1)}, u32[]{:S(2)}) copy-start(bf16[200,12288]{1,0:T(8,128)(2,1)} %slab_ref.1) | copy-start | bytes 14745604
Sparse Core Ops, SparseCore 0:
  10.7 42.6 all-gather.3

commit v2 on v1

--- a/solution.py
+++ b/solution.py
@@ -181,9 +181,49 @@
         ],
         out_specs=pl.BlockSpec((pieces, chunk, LANES), lambda i: (0, i, 0)),
         scratch_shapes=[VMEM((blocks // LANES, chunk * rows_here, LANES), jnp.float32)],
-        compiler_params=pltpu.CompilerParams(vmem_limit_bytes=40 * 2**20),
+        compiler_params=pltpu.CompilerParams(vmem_limit_bytes=58 * 2**20),
         name="transform",
     )(maps, row_table, column_table)
+
+
+def names_kernel(names_ref, all_ref, sends, recvs):
+    devices = all_ref.shape[0]
+    me = lax.axis_index("map")
+    peers = [lax.rem(me + s, devices) for s in range(1, devices)]
+    barrier = pltpu.get_barrier_semaphore()
+    for peer in peers:
+        pl.semaphore_signal(barrier, inc=1, device_id={"map": peer}, device_id_type=MESH)
+    pl.semaphore_wait(barrier, devices - 1)
+    copies = []
+    for s, peer in enumerate(peers):
+        copy = pltpu.make_async_remote_copy(
+            src_ref=names_ref,
+            dst_ref=all_ref.at[me],
+            send_sem=sends.at[s],
+            recv_sem=recvs.at[s],
+            device_id={"map": peer},
+            device_id_type=MESH,
+        )
+        copy.start()
+        copies.append(copy)
+    all_ref[me] = names_ref[...]
+    for copy in copies:
+        copy.wait()
+
+
+def gather_names(names, devices):
+    return pl.pallas_call(
+        names_kernel,
+        out_shape=jax.ShapeDtypeStruct((devices,) + names.shape, names.dtype),
+        in_specs=[pl.BlockSpec(memory_space=VMEM)],
+        out_specs=pl.BlockSpec(memory_space=VMEM),
+        scratch_shapes=[
+            pltpu.SemaphoreType.DMA((devices - 1,)),
+            pltpu.SemaphoreType.DMA((devices - 1,)),
+        ],
+        compiler_params=pltpu.CompilerParams(collective_id=1, has_side_effects=True),
+        name="names",
+    )(names)
 
 
 def combine_kernel(
@@ -215,32 +255,29 @@
         copy.start()
         return copy
 
+    order = (2, 1, 3, 0)
+    zs = [lax.rem(z + s, 4) for s in order]
     first = []
-    for xi in range(2):
-        xx = 1 - x if xi == 0 else x
-        for zi in range(4):
-            n = xi * 4 + zi
-            first.append(
-                send(n, part_ref.at[zi * 4 + xx * 2 + 1 - core], from_core.at[n], core_peer)
-            )
+    for n in range(8):
+        xx = 1 - x if n < 4 else x
+        piece = zs[n % 4] * 4 + xx * 2 + 1 - core
+        first.append(send(n, part_ref.at[piece], from_core.at[n], core_peer))
     second = []
     for n in range(4):
         first[n].wait_recv()
-        held[n] = part_ref[n * 4 + (1 - x) * 2 + core] + from_core[n]
+        held[n] = part_ref[zs[n] * 4 + (1 - x) * 2 + core] + from_core[n]
         second.append(send(8 + n, held.at[n], from_x.at[n], x_peer))
     third = []
-    for s in (1, 2, 3, 0):
-        zi = lax.rem(z + s, 4)
-        if s == 1:
-            for n in range(4):
-                first[4 + n].wait_recv()
-                second[n].wait_recv()
-        held[4 + s] = part_ref[zi * 4 + x * 2 + core] + from_core[4 + zi] + from_x[zi]
+    for n, s in enumerate(order):
+        first[4 + n].wait_recv()
+        own = part_ref[zs[n] * 4 + x * 2 + core] + from_core[4 + n]
+        second[n].wait_recv()
+        held[4 + n] = own + from_x[n]
         if s:
-            third.append(send(12 + s - 1, held.at[4 + s], from_z.at[s - 1], z_peers[s - 1]))
+            third.append(send(12 + n, held.at[4 + n], from_z.at[n], z_peers[s - 1]))
     for copy in third:
         copy.wait_recv()
-    total = held[4] + from_z[0] + from_z[1] + from_z[2]
+    total = held[7] + from_z[0] + from_z[1] + from_z[2]
     pad = out_ref.shape[1] - members
     mine = jnp.concatenate([total, jnp.zeros((pad, LANES), jnp.float32)], axis=0)
     out_ref[me] = mine.astype(jnp.bfloat16)
@@ -288,13 +325,21 @@
 
 
 def solve_kernel(
-    weight_scale, predicted_ref, data_ref, weights_ref, high_ref, low_ref, misfit_ref,
-    weighted, paired, system,
+    weight_scale, predicted_ref, data_ref, slab_ref, updated_ref, weights_ref, misfit_ref,
+    weighted, paired, system, slab, reads, writes,
 ):
     pieces = predicted_ref.shape[0]
     members = weights_ref.shape[0]
     halves = data_ref.shape[2] // LANES
     wide = 256
+    tiles = reads.shape[0]
+    tile = slab.shape[1] // tiles
+    fetches = []
+    for n in range(tiles):
+        here = slice(n * tile, (n + 1) * tile)
+        fetch = pltpu.make_async_copy(slab_ref.at[:, here], slab.at[:, here], reads.at[n])
+        fetch.start()
+        fetches.append(fetch)
     for n in range(pieces):
         c, half = divmod(n, halves)
         lanes = slice(half * LANES, (half + 1) * LANES)
@@ -305,13 +350,11 @@
         observed = data[members : members + 1]
         scale = data[members + 1 : members + 2]
         center = jnp.sum(predicted, axis=0, keepdims=True) / members
-        anomaly = (predicted - center) / math.sqrt(members - 1)
+        anomaly = (predicted - center) * (1.0 / math.sqrt(members - 1))
         weight = weight_scale / (scale * scale)
         mismatch = observed + math.sqrt(inflation) * scale * noise - predicted
-        relative = mismatch / scale
-        misfit_ref[c : c + 1, lanes] = jnp.sqrt(
-            jnp.sum(relative * relative, axis=0, keepdims=True) / members + epsilon
-        )
+        squares = jnp.sum(mismatch * mismatch, axis=0, keepdims=True) / (scale * scale)
+        misfit_ref[c : c + 1, lanes] = jnp.sqrt(squares / members + epsilon)
         weighted[:, here] = anomaly * weight
         paired[0:members, here] = anomaly
         paired[wide : wide + members, here] = mismatch
@@ -330,76 +373,82 @@
     width = system.shape[1]
     sub = lax.broadcasted_iota(jnp.int32, (8, 1), 0)
     row_number = lax.broadcasted_iota(jnp.int32, (members, 1), 0)
+    block = system[0:8, :]
     for k in range(members // 8):
         start = 8 * k
         low = start // LANES * LANES
-        block = system[start : start + 8, low:width]
         for j in range(8):
             at = start - low + j
             column = block[:, at : at + 1]
-            pivot = block[j : j + 1, :] / column[j : j + 1, :]
+            pivot = block[j : j + 1, :] * (1.0 / column[j : j + 1, :])
             block = jnp.where(sub == j, pivot, block - column * pivot)
         columns = system[:, start : start + 8]
+        after = None
+        if start + 8 < members:
+            after = system[start + 8 : start + 16, low:width]
+            terms = [columns[start + 8 : start + 16, j : j + 1] * block[j : j + 1, :] for j in range(8)]
+            after = after - (
+                ((terms[0] + terms[1]) + (terms[2] + terms[3]))
+                + ((terms[4] + terms[5]) + (terms[6] + terms[7]))
+            )
+            after = after[:, (start + 8) // LANES * LANES - low :]
         outside = (row_number < start) | (row_number >= start + 8)
         columns = jnp.where(outside, columns, 0.0)
         system[:, low:width] = system[:, low:width] - jnp.dot(
             columns, block, preferred_element_type=jnp.float32, precision=lax.Precision.HIGHEST
         )
         system[start : start + 8, low:width] = block
+        block = after
     solved = system[:, wide : wide + members]
     weights_ref[...] = solved
     centred = (solved - jnp.sum(solved, axis=0, keepdims=True) / members) / math.sqrt(members - 1)
     turned = centred.T
     high = turned.astype(jnp.bfloat16)
-    high_ref[...] = high
-    low_ref[...] = (turned - high.astype(jnp.float32)).astype(jnp.bfloat16)
-
-
-def solve(predicted, data, members, weight_scale):
+    low_part = (turned - high.astype(jnp.float32)).astype(jnp.bfloat16)
+    stores = []
+    for n in range(tiles):
+        here = slice(n * tile, (n + 1) * tile)
+        fetches[n].wait()
+        state = slab[:, here]
+        moved = jnp.dot(high, state, preferred_element_type=jnp.float32)
+        moved = moved + jnp.dot(low_part, state, preferred_element_type=jnp.float32)
+        slab[:, here] = (state.astype(jnp.float32) + moved).astype(jnp.bfloat16)
+        store = pltpu.make_async_copy(slab.at[:, here], updated_ref.at[:, here], writes.at[n])
+        store.start()
+        stores.append(store)
+    for store in stores:
+        store.wait()
+
+
+def solve(predicted, data, slab, weight_scale):
     pieces = predicted.shape[0]
+    members, here = slab.shape
     cells = pieces * LANES
-    square = (members, members)
+    tiles = 12
     return pl.pallas_call(
         functools.partial(solve_kernel, weight_scale),
         out_shape=(
-            jax.ShapeDtypeStruct(square, jnp.float32),
-            jax.ShapeDtypeStruct(square, jnp.bfloat16),
-            jax.ShapeDtypeStruct(square, jnp.bfloat16),
+            jax.ShapeDtypeStruct(slab.shape, jnp.bfloat16),
+            jax.ShapeDtypeStruct((members, members), jnp.float32),
             jax.ShapeDtypeStruct((data.shape[0], data.shape[2]), jnp.float32),
         ),
-        in_specs=[pl.BlockSpec(memory_space=VMEM)] * 2,
-        out_specs=(pl.BlockSpec(memory_space=VMEM),) * 4,
+        in_specs=[pl.BlockSpec(memory_space=VMEM)] * 2 + [pl.BlockSpec(memory_space=pltpu.HBM)],
+        out_specs=(
+            pl.BlockSpec(memory_space=pltpu.HBM),
+            pl.BlockSpec(memory_space=VMEM),
+            pl.BlockSpec(memory_space=VMEM),
+        ),
         scratch_shapes=[
             VMEM((members, cells), jnp.float32),
             VMEM((256 + members, cells), jnp.float32),
             VMEM((members, 512), jnp.float32),
+            VMEM((members, here), jnp.bfloat16),
+            pltpu.SemaphoreType.DMA((tiles,)),
+            pltpu.SemaphoreType.DMA((tiles,)),
         ],
-        compiler_params=pltpu.CompilerParams(vmem_limit_bytes=40 * 2**20),
+        compiler_params=pltpu.CompilerParams(vmem_limit_bytes=58 * 2**20),
         name="solve",
-    )(predicted, data)
-
-
-def update_kernel(high_ref, low_ref, slab_ref, out_ref):
-    state = slab_ref[...]
-    moved = jnp.dot(high_ref[...], state, preferred_element_type=jnp.float32)
-    moved = moved + jnp.dot(low_ref[...], state, preferred_element_type=jnp.float32)
-    out_ref[...] = (state.astype(jnp.float32) + moved).astype(jnp.bfloat16)
-
-
-def update(high, low, slab):
-    members, cells = slab.shape
-    tile = 1024
-    whole = pl.BlockSpec((members, members), lambda i: (0, 0))
-    column = pl.BlockSpec((members, tile), lambda i: (0, i))
-    return pl.pallas_call(
-        update_kernel,
-        grid=(cells // tile,),
-        out_shape=jax.ShapeDtypeStruct(slab.shape, jnp.bfloat16),
-        in_specs=[whole, whole, column],
-        out_specs=column,
-        compiler_params=pltpu.CompilerParams(vmem_limit_bytes=40 * 2**20),
-        name="update",
-    )(high, low, slab)
+    )(predicted, data, slab)
 
 
 def body_small(amplitude_maps, kept_blocks, block_owner, observed, error_scale, perturbation, model_slab):
@@ -414,7 +463,8 @@
     table_h = jnp.asarray(dct_constant(map_height))
 
     names = jnp.stack([kept_blocks, block_owner[:, 0]])
-    names = lax.all_gather(names, "map")
+    names = jnp.pad(names, ((0, 6), (0, LANES - keep_count)))
+    names = gather_names(names, devices)[:, :, :keep_count]
     local = jnp.concatenate(
         [perturbation, observed[:, None], error_scale[:, None]], axis=1
     )
@@ -454,8 +504,7 @@
         preferred_element_type=jnp.float32,
     ).astype(one)
     weight_scale = members / (devices * keep_count * BLK)
-    update_weights, high, low, misfit = solve(predicted, data, members, weight_scale)
-    updated_slab = update(high, low, model_slab)
+    updated_slab, update_weights, misfit = solve(predicted, data, model_slab, weight_scale)
     mine = lax.dynamic_slice_in_dim(pick_slot, me * devices * CAP, devices * CAP, axis=0)
     data_misfit = jnp.einsum(
         "sb,cb->sc", mine.astype(jnp.float32), misfit, precision=lax.Precision.HIGHEST

time: 138 us -> 115 us (0.83)
  blocking collectives: 23.1 us -> 0 us
  matrix products: 2.88 us -> 5.87 us
  local copies, waits for them, and re-layouts: 12.1 us -> 9.74 us
  Pallas kernels: 82.7 us -> 81.2 us
    all_gather x1 -> x0, blocking collectives: 23.1 us -> none  [body_small(): names = lax.all_gather(names, 'map')]
    pallas_call x1, Pallas kernels: 34.6 us -> 29.7 us  [combine(): pl.pallas_call(combine_kernel, out_shape=jax.ShapeDtypeStruct((pieces, pa...]
    unnamed x4, local copies, waits for them, and re-layouts: 5.32 us -> 2.31 us
    pallas_call x1, Pallas kernels: 7.41 us -> 10.1 us  [gather_names(): pl.pallas_call(names_kernel, out_shape=jax.ShapeDtypeStruct((devices,) +...]
    pallas_call x1, Pallas kernels: 10.4 us -> 12.5 us  [transform(): pl.pallas_call(functools.partial(transform_kernel, rows_here), grid=(memb...]
    pallas_call x1, Pallas kernels: 30.3 us -> 28.8 us  [solve(): pl.pallas_call(functools.partial(solve_kernel, weight_scale), out_shape=(...]
  transfers between devices with their start and end apart: 1 -> 1, of which waited for: 0 -> 0; matrix products, arithmetic and copies ran while one was open for 3% -> 6% of each run, Pallas kernels for 33% -> 46%
where the time goes in v2:
time: 115 us
  Pallas kernels  81.2 us (71%)
  between operations  14.1 us (12%)
  local copies, waits for them, and re-layouts  9.74 us (8%)
  matrix products  5.87 us (5%)
  other arithmetic  3.72 us (3%)
    pallas_call x1, Pallas kernels, combine(): pl.pallas_call(combine_kernel, out_shape=jax.ShapeDtypeStruct((pieces, pa...  29.7 us
    pallas_call x1, Pallas kernels, solve(): pl.pallas_call(functools.partial(solve_kernel, weight_scale), out_shape=(...  28.8 us
    pallas_call x1, Pallas kernels, transform(): pl.pallas_call(functools.partial(transform_kernel, rows_here), grid=(memb...  12.5 us
    pallas_call x1, Pallas kernels, gather_names(): pl.pallas_call(names_kernel, out_shape=jax.ShapeDtypeStruct((devices,) +...  10.1 us
    all_gather x1, local copies, waits for them, and re-layouts, body_small(): local = lax.all_gather(local, 'map', tiled=True)  3.37 us
    unnamed x4, local copies, waits for them, and re-layouts  2.31 us
  transfers between devices with their start and end apart: 1, of which 0 were waited for; matrix products, arithmetic and copies ran while one was open for 6% of the time, Pallas kernels for 46%

profile of v2, /device:TPU:0, one launch (start us, length us, event | category | flops | bytes accessed | tf_op | source)
XLA Modules:
  0.0 114.7 jit_solution(3901803172642669905)
XLA Ops:
  7.2 0.7 broadcast_in_dim.10
  7.9 0.7 broadcast_in_dim.9
  8.5 1.5 %pad_maximum_fusion = bf16[256,202]{0,1:T(8,128)(2,1)} fusion(bf16[256,1]{0,1:T(2,128)(2,1)S(1)} %broadcast_in_dim.10, bf16[256,1]{0,1:T(2,128)(2,1)S(1)} %broadcast_in_dim.9, bf16[256,200]{0,1:T(8,128)(2,1)} %param.14), kind=kLoop, calls=%fused_computation.11 | loop fusion | flops 310272 | bytes 206848 | tf_op jit(solution)/shard_map/concatenate | solution.py:468
  10.1 0.7 pad_add_fusion
  10.8 0.6 pad.4.names_ref
  11.4 10.1 %names.1 = s32[16,8,128]{2,1,0:T(8,128)} custom-call(s32[8,128]{1,0:T(8,128)} %pad.4.names_ref), custom_call_target="tpu_custom_call" | custom-call | tf_op jit(solution)/shard_map/names/pallas_call | solution.py:215
  21.5 1.0 multiply_reduce_fusion
  22.5 0.4 convert_reduce_fusion
  23.0 0.1 mul.43
  23.1 0.1 reshape_squeeze.3
  23.2 1.0 dynamic-slice_bitcast_fusion
  24.3 0.1 copy.18
  24.4 0.9 convolution_bitcast_fusion.column_table_ref
  25.3 2.1 %convolution_convert_fusion.row_table_ref = bf16[256,512]{1,0:T(8,128)(2,1)} fusion(bf16[512,512]{1,0:T(8,128)(2,1)} %constant.47.clone, s32[256]{0:T(256)S(1)} %get-tuple-element.13), kind=kOutput, calls=%fused_computation.3 | convolution fusion | flops 134479872 | bytes 787456 | tf_op jit(solution)/shard_map/dot_general | solution.py:480
  27.4 12.5 %transform.1.part_ref = f32[16,200,128]{2,1,0:T(8,128)} custom-call(bf16[200,32,512]{2,1,0:T(8,128)(2,1)} %maps_ref.1, bf16[256,512]{1,0:T(8,128)(2,1)} %convolution_convert_fusion.row_table_ref, f32[32,8,256]{2,1,0:T(8,128)} %convolution_bitcast_fusion.column_table_ref), custom_call_target="tpu_custom_call" | custom-call | tf_op jit(solution)/shard_map/transform/pallas_call | solution.py:173
  39.9 1.4 %copy-done = f32[16,200,128]{2,1,0:T(8,128)S(1)} copy-done((f32[16,200,128]{2,1,0:T(8,128)S(1)}, f32[16,200,128]{2,1,0:T(8,128)}, u32[]{:S(2)}) %copy-start) | copy-done | bytes 1638424
  41.3 29.7 %combine.1.predicted_ref = bf16[16,208,128]{2,1,0:T(8,128)(2,1)S(1)} custom-call(f32[16,200,128]{2,1,0:T(8,128)S(1)} %copy-done), custom_call_target="tpu_custom_call" | custom-call | tf_op jit(solution)/shard_map/combine/pallas_call | solution.py:307
  71.1 0.9 copy-done.1
  71.9 0.1 iota_compare_fusion
  72.1 3.4 %copy.19 = bf16[4096,202]{1,0:T(8,128)(2,1)S(1)} copy(bf16[4096,202]{0,1:T(8,128)(2,1)} %all-gather.2.cloned.1.call-done) | data formatting | bytes 3309568 | tf_op jit(solution)/shard_map/all_gather | solution.py:471
  75.4 2.1 %fusion.2.data_ref = bf16[8,202,256]{2,1,0:T(8,128)(2,1)} fusion(bf16[512,8,202]{2,1,0:T(8,128)(2,1)S(1)} %bitcast.17, s32[256]{0:T(256)S(1)} %get-tuple-element.12), kind=kOutput, calls=%fused_computation.2 | convolution fusion | flops 424169472 | bytes 2483200 | tf_op jit(solution)/shard_map/sce,sb->ceb/dot_general | solution.py:500
  77.5 28.8 %solve.1 = (bf16[200,12288]{1,0:T(8,128)(2,1)}, f32[200,200]{1,0:T(8,128)}, f32[8,256]{1,0:T(8,128)}) custom-call(bf16[16,208,128]{2,1,0:T(8,128)(2,1)} %copy-done.1, bf16[8,202,256]{2,1,0:T(8,128)(2,1)} %fusion.2.data_ref, bf16[200,12288]{1,0:T(8,128)(2,1)} %slab_ref.1), custom_call_target="tpu_custom_call" | custom-call | tf_op jit(solution)/shard_map/solve/pallas_call | solution.py:428
  106.4 0.8 fusion.10
  107.2 0.7 reshape.114
  (10 shorter events, 0.3 us)
Async XLA Ops:
  7.2 64.9 %all-gather.2.cloned.1.call-start = ((), (), s32[]{:S(2)}) async-start(), calls=%async_computation | async-start | bytes 1810432 | tf_op jit(solution)/shard_map/all_gather | solution.py:471
  39.9 1.4 %copy-start = (f32[16,200,128]{2,1,0:T(8,128)S(1)}, f32[16,200,128]{2,1,0:T(8,128)}, u32[]{:S(2)}) copy-start(f32[16,200,128]{2,1,0:T(8,128)} %transform.1.part_ref) | copy-start | bytes 4915204
  71.1 0.9 copy-start.1
Sparse Core Ops, SparseCore 0:
  10.7 42.2 all-gather.1

commit v3 on v2

--- a/solution.py
+++ b/solution.py
@@ -148,21 +148,23 @@
     for half in range(halves):
         rowwise_ref[half] = rowwise[:, half * LANES : (half + 1) * LANES]
 
-    def tile(t, carry):
-        for half in range(halves):
-            lanes = slice(half * LANES, (half + 1) * LANES)
-            total = [None] * BLK
-            for h in range(rows_here):
+    tiles = range(chunk // 8)
+    for half in range(halves):
+        lanes = slice(half * LANES, (half + 1) * LANES)
+        total = [[None] * BLK for _ in tiles]
+        for h in range(rows_here):
+            rows = []
+            for t in tiles:
                 row = rowwise_ref[half, pl.ds(t * 8 * rows_here + h, 8, stride=rows_here), :]
-                row = row.astype(jnp.bfloat16).astype(jnp.float32)
-                for c in range(BLK):
-                    term = row * column_table_ref[h, c : c + 1, lanes]
-                    total[c] = term if total[c] is None else total[c] + term
+                rows.append(row.astype(jnp.bfloat16).astype(jnp.float32))
             for c in range(BLK):
-                part_ref[c * halves + half, pl.ds(pl.multiple_of(t * 8, 8), 8), :] = total[c]
-        return carry
-
-    lax.fori_loop(0, chunk // 8, tile, 0)
+                entry = column_table_ref[h, c : c + 1, lanes]
+                for t in tiles:
+                    term = rows[t] * entry
+                    total[t][c] = term if h == 0 else total[t][c] + term
+        for t in tiles:
+            for c in range(BLK):
+                part_ref[c * halves + half, t * 8 : t * 8 + 8, :] = total[t][c]
 
 
 def transform(maps, row_table, column_table):
@@ -358,46 +360,42 @@
         weighted[:, here] = anomaly * weight
         paired[0:members, here] = anomaly
         paired[wide : wide + members, here] = mismatch
-    contract = (((1,), (1,)), ((), ()))
-    for part in range(2):
-        rows = slice(part * wide, part * wide + members)
-        product = lax.dot_general(
-            weighted[...], paired[rows, :], contract,
-            preferred_element_type=jnp.float32, precision=lax.Precision.HIGHEST,
-        )
-        if part == 0:
-            i = lax.broadcasted_iota(jnp.int32, product.shape, 0)
-            j = lax.broadcasted_iota(jnp.int32, product.shape, 1)
-            product = product + jnp.where(i == j, inflation, 0.0)
-        system[:, part * wide : part * wide + members] = product
+    paired[members:wide, :] = jnp.zeros((wide - members, paired.shape[1]), jnp.float32)
+    product = lax.dot_general(
+        weighted[...], paired[...], (((1,), (1,)), ((), ())),
+        preferred_element_type=jnp.float32, precision=lax.Precision.HIGHEST,
+    )
+    i = lax.broadcasted_iota(jnp.int32, product.shape, 0)
+    j = lax.broadcasted_iota(jnp.int32, product.shape, 1)
+    system[:, 0 : wide + members] = product + jnp.where(i == j, inflation, 0.0)
     width = system.shape[1]
-    sub = lax.broadcasted_iota(jnp.int32, (8, 1), 0)
+    size = 16
     row_number = lax.broadcasted_iota(jnp.int32, (members, 1), 0)
-    block = system[0:8, :]
-    for k in range(members // 8):
-        start = 8 * k
+    block = system[0:size, :]
+    for start in range(0, members, size):
         low = start // LANES * LANES
-        for j in range(8):
+        stop = min(start + size, members)
+        sub = lax.broadcasted_iota(jnp.int32, (stop - start, 1), 0)
+        for j in range(stop - start):
             at = start - low + j
             column = block[:, at : at + 1]
             pivot = block[j : j + 1, :] * (1.0 / column[j : j + 1, :])
             block = jnp.where(sub == j, pivot, block - column * pivot)
-        columns = system[:, start : start + 8]
+        columns = system[:, start:stop]
         after = None
-        if start + 8 < members:
-            after = system[start + 8 : start + 16, low:width]
-            terms = [columns[start + 8 : start + 16, j : j + 1] * block[j : j + 1, :] for j in range(8)]
-            after = after - (
-                ((terms[0] + terms[1]) + (terms[2] + terms[3]))
-                + ((terms[4] + terms[5]) + (terms[6] + terms[7]))
-            )
-            after = after[:, (start + 8) // LANES * LANES - low :]
-        outside = (row_number < start) | (row_number >= start + 8)
+        if stop < members:
+            end = min(stop + size, members)
+            after = system[stop:end, low:width]
+            terms = [columns[stop:end, j : j + 1] * block[j : j + 1, :] for j in range(stop - start)]
+            while len(terms) > 1:
+                terms = [terms[n] + terms[n + 1] for n in range(0, len(terms), 2)]
+            after = (after - terms[0])[:, stop // LANES * LANES - low :]
+        outside = (row_number < start) | (row_number >= stop)
         columns = jnp.where(outside, columns, 0.0)
         system[:, low:width] = system[:, low:width] - jnp.dot(
             columns, block, preferred_element_type=jnp.float32, precision=lax.Precision.HIGHEST
         )
-        system[start : start + 8, low:width] = block
+        system[start:stop, low:width] = block
         block = after
     solved = system[:, wide : wide + members]
     weights_ref[...] = solved

time: 115 us -> 113 us (0.983)
  Pallas kernels: 81.2 us -> 79.4 us
    pallas_call x1, Pallas kernels: 28.8 us -> 27.1 us  [solve(): pl.pallas_call(functools.partial(solve_kernel, weight_scale), out_shape=(...]
where the time goes in v3:
time: 113 us
  Pallas kernels  79.4 us (70%)
  between operations  14.1 us (12%)
  local copies, waits for them, and re-layouts  9.74 us (9%)
  matrix products  5.88 us (5%)
  other arithmetic  3.72 us (3%)
    pallas_call x1, Pallas kernels, combine(): pl.pallas_call(combine_kernel, out_shape=jax.ShapeDtypeStruct((pieces, pa...  29.7 us
    pallas_call x1, Pallas kernels, solve(): pl.pallas_call(functools.partial(solve_kernel, weight_scale), out_shape=(...  27.1 us
    pallas_call x1, Pallas kernels, transform(): pl.pallas_call(functools.partial(transform_kernel, rows_here), grid=(memb...  12.5 us
    pallas_call x1, Pallas kernels, gather_names(): pl.pallas_call(names_kernel, out_shape=jax.ShapeDtypeStruct((devices,) +...  10.1 us
    all_gather x1, local copies, waits for them, and re-layouts, body_small(): local = lax.all_gather(local, 'map', tiled=True)  3.37 us
    unnamed x4, local copies, waits for them, and re-layouts  2.31 us
  transfers between devices with their start and end apart: 1, of which 0 were waited for; matrix products, arithmetic and copies ran while one was open for 6% of the time, Pallas kernels for 46%

profile of v3, /device:TPU:0, one launch (start us, length us, event | category | flops | bytes accessed | tf_op | source)
XLA Modules:
  0.0 112.9 jit_solution(18030314880145301618)
XLA Ops:
  7.2 0.7 broadcast_in_dim.10
  7.9 0.7 broadcast_in_dim.9
  8.5 1.5 %pad_maximum_fusion = bf16[256,202]{0,1:T(8,128)(2,1)} fusion(bf16[256,1]{0,1:T(2,128)(2,1)S(1)} %broadcast_in_dim.10, bf16[256,1]{0,1:T(2,128)(2,1)S(1)} %broadcast_in_dim.9, bf16[256,200]{0,1:T(8,128)(2,1)} %param.14), kind=kLoop, calls=%fused_computation.11 | loop fusion | flops 310272 | bytes 206848 | tf_op jit(solution)/shard_map/concatenate | solution.py:466
  10.1 0.7 pad_add_fusion
  10.8 0.6 pad.4.names_ref
  11.4 10.1 %names.1 = s32[16,8,128]{2,1,0:T(8,128)} custom-call(s32[8,128]{1,0:T(8,128)} %pad.4.names_ref), custom_call_target="tpu_custom_call" | custom-call | tf_op jit(solution)/shard_map/names/pallas_call | solution.py:217
  21.5 1.0 multiply_reduce_fusion
  22.5 0.4 convert_reduce_fusion
  23.0 0.1 mul.43
  23.1 0.1 reshape_squeeze.3
  23.2 1.0 dynamic-slice_bitcast_fusion
  24.3 0.1 copy.18
  24.4 0.9 convolution_bitcast_fusion.column_table_ref
  25.3 2.1 %convolution_convert_fusion.row_table_ref = bf16[256,512]{1,0:T(8,128)(2,1)} fusion(bf16[512,512]{1,0:T(8,128)(2,1)} %constant.47.clone, s32[256]{0:T(256)S(1)} %get-tuple-element.13), kind=kOutput, calls=%fused_computation.3 | convolution fusion | flops 134479872 | bytes 787456 | tf_op jit(solution)/shard_map/dot_general | solution.py:478
  27.4 12.5 %transform.1.part_ref = f32[16,200,128]{2,1,0:T(8,128)} custom-call(bf16[200,32,512]{2,1,0:T(8,128)(2,1)} %maps_ref.1, bf16[256,512]{1,0:T(8,128)(2,1)} %convolution_convert_fusion.row_table_ref, f32[32,8,256]{2,1,0:T(8,128)} %convolution_bitcast_fusion.column_table_ref), custom_call_target="tpu_custom_call" | custom-call | tf_op jit(solution)/shard_map/transform/pallas_call | solution.py:175
  39.9 1.4 %copy-done = f32[16,200,128]{2,1,0:T(8,128)S(1)} copy-done((f32[16,200,128]{2,1,0:T(8,128)S(1)}, f32[16,200,128]{2,1,0:T(8,128)}, u32[]{:S(2)}) %copy-start) | copy-done | bytes 1638424
  41.3 29.7 %combine.1.predicted_ref = bf16[16,208,128]{2,1,0:T(8,128)(2,1)S(1)} custom-call(f32[16,200,128]{2,1,0:T(8,128)S(1)} %copy-done), custom_call_target="tpu_custom_call" | custom-call | tf_op jit(solution)/shard_map/combine/pallas_call | solution.py:309
  71.0 0.9 copy-done.1
  71.9 0.1 iota_compare_fusion
  72.0 3.4 %copy.19 = bf16[4096,202]{1,0:T(8,128)(2,1)S(1)} copy(bf16[4096,202]{0,1:T(8,128)(2,1)} %all-gather.2.cloned.1.call-done) | data formatting | bytes 3309568 | tf_op jit(solution)/shard_map/all_gather | solution.py:469
  75.4 2.1 %fusion.2.data_ref = bf16[8,202,256]{2,1,0:T(8,128)(2,1)} fusion(bf16[512,8,202]{2,1,0:T(8,128)(2,1)S(1)} %bitcast.17, s32[256]{0:T(256)S(1)} %get-tuple-element.12), kind=kOutput, calls=%fused_computation.2 | convolution fusion | flops 424169472 | bytes 2483200 | tf_op jit(solution)/shard_map/sce,sb->ceb/dot_general | solution.py:498
  77.5 27.1 %solve.1 = (bf16[200,12288]{1,0:T(8,128)(2,1)}, f32[200,200]{1,0:T(8,128)}, f32[8,256]{1,0:T(8,128)}) custom-call(bf16[16,208,128]{2,1,0:T(8,128)(2,1)} %copy-done.1, bf16[8,202,256]{2,1,0:T(8,128)(2,1)} %fusion.2.data_ref, bf16[200,12288]{1,0:T(8,128)(2,1)} %slab_ref.1), custom_call_target="tpu_custom_call" | custom-call | tf_op jit(solution)/shard_map/solve/pallas_call | solution.py:426
  104.6 0.8 fusion.10
  105.4 0.7 reshape.114
  (10 shorter events, 0.3 us)
Async XLA Ops:
  7.2 64.8 %all-gather.2.cloned.1.call-start = ((), (), s32[]{:S(2)}) async-start(), calls=%async_computation | async-start | bytes 1810432 | tf_op jit(solution)/shard_map/all_gather | solution.py:469
  39.9 1.4 %copy-start = (f32[16,200,128]{2,1,0:T(8,128)S(1)}, f32[16,200,128]{2,1,0:T(8,128)}, u32[]{:S(2)}) copy-start(f32[16,200,128]{2,1,0:T(8,128)} %transform.1.part_ref) | copy-start | bytes 4915204
  71.0 0.9 copy-start.1
Sparse Core Ops, SparseCore 0:
  10.7 42.2 all-gather.1
